TPU v7x, 32 devices: a whole 2x2x4 slice. The times are simulated.
32 devices in a mesh: ctx: 16 (over z, x, core), head: 2 (over y).
Axes of the slice: x: 2, y: 2, z: 4, core: 2. Of those that a mesh axis runs over, the one named last changes fastest.
Arguments:
- mixer_input: bfloat16 [8192, 4096], P('ctx', 'head'), may hold values from -61 to 61
- gate_input: bfloat16 [8192, 4096], P('ctx', 'head'), may hold values from -7.5 to 7.5
- write_vecs: bfloat16 [8192, 128], P('ctx'), may hold values from -0.8984375 to 0.8984375
- read_vecs: bfloat16 [8192, 128], P('ctx'), may hold values from -0.8984375 to 0.8984375
- log_decay: float32 [64, 8192], P('head', 'ctx'), may hold values from -0.76 to 0
- doc_start: int32 [8192], P('ctx'), may hold values from 0 to 1, as said below
- live_mask: int32 [8192], P('ctx'), may hold values from 0 to 1, as said below
- skip_gain: float32 [64], P('head'), may hold values from 0.5 to 2
- norm_gain: float32 [4096], P('head'), may hold values from 0.25 to 1.75
- residual: bfloat16 [8192, 2048], P('ctx', 'head'), may hold values from -61 to 61
- out_weight: bfloat16 [4096, 2048], P(('head', 'ctx')), may hold values from -0.09375 to 0.09375
- mlp_gain: float32 [2048], replicated, may hold values from 0.25 to 1.75
- gate_weight: bfloat16 [2048, 4096], P('ctx', 'head'), may hold values from -0.125 to 0.125
- up_weight: bfloat16 [2048, 4096], P('ctx', 'head'), may hold values from -0.125 to 0.125
- down_weight: bfloat16 [4096, 2048], P(('head', 'ctx')), may hold values from -0.09375 to 0.09375
Outputs:
- mixed: bfloat16 [8192, 2048], P('ctx', 'head')
Inputs may be any that keep to these rules, and one draw needn't show every extreme that they name: `doc_start`: documents begin only at the first token of a group of 256; the window's first token begins one; a document spans at most 16 groups, and some document spans exactly that many. `live_mask`: the 0 entries are the tokens after a document's last real token, all within its last group; every document has a real token.
All inputs are finite; a program needn't handle non-finite values.
Results may differ from a plain program's by a relative error of at most 0.007.
Values may be sent and summed in bfloat16 or wider, within the bound.
A program may use at most 128 MiB of HBM per device.

v0:
```python
import jax
import jax.numpy as jnp
from jax import lax
from jax.sharding import PartitionSpec as P

HDIM = 64
STATE = 128
GROUP = 256
INNER = 4096


EPS = 1e-05


def carried_in(part, axis, combine, identity):
    place = lax.axis_index(axis)
    gathered = jax.tree.map(lambda a: lax.all_gather(a, axis), part)
    state = jax.tree.map(lambda a, e: jnp.zeros_like(a) + jnp.asarray(e, a.dtype), part, identity)

    def one(lap, state):
        return combine(
            state, jax.tree.map(lambda a: lax.dynamic_index_in_dim(a, lap, 0, False), gathered)
        )

    return lax.fori_loop(0, place, one, state)


def group_core(masked, write_group, read_group, log_group, start_group, skip_gain):
    positions = jnp.arange(GROUP)
    log_sums = jnp.cumsum(log_group, axis=1)
    doc_index = jnp.cumsum(start_group)
    same_doc = (doc_index[:, None] == doc_index[None, :]) & (
        positions[:, None] >= positions[None, :]
    )
    scores = jnp.dot(read_group, write_group.T, preferred_element_type=jnp.float32)
    log_gaps = jnp.where(same_doc[None], log_sums[:, :, None] - log_sums[:, None, :], 0.0)
    weights = jnp.where(same_doc[None], scores[None] * jnp.exp(log_gaps), 0.0).astype(jnp.bfloat16)
    per_head = masked.reshape(GROUP, -1, HDIM)
    intra_out = jnp.einsum("hij,jhp->ihp", weights, per_head, preferred_element_type=jnp.float32)
    tail_wts = (
        jnp.exp(log_sums[:, -1:] - log_sums)
        * (doc_index == doc_index[-1]).astype(jnp.float32)[None]
    )
    weighted = (write_group.astype(jnp.float32)[None] * tail_wts[:, :, None]).astype(jnp.bfloat16)
    local_state = jnp.einsum("hjn,jhp->hnp", weighted, per_head, preferred_element_type=jnp.float32)
    reach_wts = jnp.exp(log_sums) * (doc_index == 0).astype(jnp.float32)[None]
    decay_all = jnp.exp(log_sums[:, -1]) * (doc_index[-1] == 0).astype(jnp.float32)
    direct = intra_out + skip_gain[None, :, None] * per_head.astype(jnp.float32)
    return (direct, local_state, reach_wts, decay_all)


def combine_states(earlier, latter):
    return (earlier[0] * latter[0], latter[0][:, None, None] * earlier[1] + latter[1])


def shards(
    mixer_input,
    gate_input,
    write_vecs,
    read_vecs,
    log_decay,
    doc_start,
    live_mask,
    skip_gain,
    norm_gain,
    residual,
    out_weight,
    mlp_gain,
    gate_weight,
    up_weight,
    down_weight,
):
    tok_rows = mixer_input.shape[0]
    group_total = tok_rows // GROUP
    head_count = log_decay.shape[0]
    masked = mixer_input * live_mask.astype(jnp.bfloat16)[:, None]
    read_groups = read_vecs.reshape(group_total, GROUP, -1)
    group_data = (
        masked.reshape(group_total, GROUP, -1),
        write_vecs.reshape(group_total, GROUP, -1),
        read_groups,
        log_decay.reshape(head_count, group_total, GROUP).transpose(1, 0, 2),
        doc_start.reshape(group_total, GROUP),
    )

    def group_step(pieces):
        return group_core(pieces[0], pieces[1], pieces[2], pieces[3], pieces[4], skip_gain)

    directs, local_parts, reaches, decays = lax.map(group_step, group_data)
    run_state = jnp.zeros((head_count, STATE, HDIM), jnp.float32)
    run_factor = jnp.ones((head_count,), jnp.float32)
    before = []
    factors = []
    for group_id in range(group_total):
        before.append(run_state)
        factors.append(run_factor)
        run_state = decays[group_id][:, None, None] * run_state + local_parts[group_id]
        run_factor = run_factor * decays[group_id]
    identity = (
        jnp.ones((head_count,), jnp.float32),
        jnp.zeros((head_count, STATE, HDIM), jnp.float32),
    )
    incoming = carried_in((run_factor, run_state), "ctx", combine_states, identity)[1]
    outputs = []
    for group_id in range(group_total):
        inner_state = (factors[group_id][:, None, None] * incoming + before[group_id]).astype(
            jnp.bfloat16
        )
        crossed = jnp.einsum(
            "in,hnp->ihp", read_groups[group_id], inner_state, preferred_element_type=jnp.float32
        )
        outputs.append(directs[group_id] + crossed * reaches[group_id].T[:, :, None])
    output = jnp.concatenate(outputs, axis=0).reshape(tok_rows, -1)
    gated = output * jax.nn.silu(gate_input.astype(jnp.float32))
    squares = lax.psum(jnp.sum(gated * gated, axis=1), "head")
    normed = (gated * lax.rsqrt(squares / INNER + EPS)[:, None] * norm_gain).astype(jnp.bfloat16)
    width = out_weight.shape[1]
    columns = normed
    projected = jnp.dot(
        columns,
        lax.all_gather(out_weight, "ctx", axis=0, tiled=True),
        preferred_element_type=jnp.float32,
    )
    slice_width = residual.shape[1]
    offset = lax.axis_index("head") * slice_width
    placed = lax.dynamic_update_slice_in_dim(
        jnp.zeros((tok_rows, width), jnp.float32), residual.astype(jnp.float32), offset, 1
    )
    hidden_full = lax.psum(projected + placed, "head").astype(jnp.bfloat16)
    hidden_wide = hidden_full.astype(jnp.float32)
    row_scale = lax.rsqrt(jnp.mean(hidden_wide * hidden_wide, axis=1) + EPS)
    scaled = (hidden_wide * row_scale[:, None] * mlp_gain).astype(jnp.bfloat16)
    hidden = lax.dynamic_slice_in_dim(hidden_full, offset, slice_width, 1)
    pieces = (
        lax.all_gather(gate_weight, "ctx", axis=0, tiled=True),
        lax.all_gather(up_weight, "ctx", axis=0, tiled=True),
    )
    columns = scaled
    gate_out = jnp.dot(columns, pieces[0], preferred_element_type=jnp.float32)
    up_out = jnp.dot(columns, pieces[1], preferred_element_type=jnp.float32)
    act = (jax.nn.silu(gate_out) * up_out).astype(jnp.bfloat16)
    columns = act
    down_out = jnp.dot(
        columns,
        lax.all_gather(down_weight, "ctx", axis=0, tiled=True),
        preferred_element_type=jnp.float32,
    )
    mlp_part = lax.psum_scatter(
        down_out.astype(jnp.bfloat16), "head", scatter_dimension=1, tiled=True
    ).astype(jnp.float32)
    return (
        live_mask.astype(jnp.float32)[:, None] * (hidden.astype(jnp.float32) + mlp_part)
    ).astype(jnp.bfloat16)


def solution(mesh):
    return jax.shard_map(
        shards,
        mesh=mesh,
        in_specs=(
            P("ctx", "head"),
            P("ctx", "head"),
            P("ctx", None),
            P("ctx", None),
            P("head", "ctx"),
            P("ctx"),
            P("ctx"),
            P("head"),
            P("head"),
            P("ctx", "head"),
            P(("head", "ctx"), None),
            P(),
            P("ctx", "head"),
            P("ctx", "head"),
            P(("head", "ctx"), None),
        ),
        out_specs=P("ctx", "head"),
        check_vma=False,
    )
```

profile of v0, /device:TPU:0, one launch (start us, length us, event | category | flops | bytes accessed | tf_op | source)
XLA Modules:
  0.0 536.5 jit_solution(12506320130966027330)
XLA Ops:
  6.5 0.8 fusion.45
  7.3 1.5 reshape.277
  8.8 0.7 reshape.274
  9.5 3.1 broadcast_multiply_fusion
  12.7 33.1 %while.28 = (s32[]{:T(128)}, f32[2,256,32,64]{1,3,2,0:T(8,128)}, f32[2,32,128,64]{2,3,1,0:T(8,128)}, f32[2,32,256]{2,1,0:T(8,128)}, f32[2,32]{1,0:T(2,128)S(1)},...) while((s32[]{:T(128)}, f32[2,256,32,64]{1,3,2,0:T(8,128)}, ...), condition=%wide.region_5.6_spmd, body=%wide.region_0.5_spmd.sunk | while | flops 434922624 | bytes 29115836 | solution.py:89
  12.7 0.9 constant_dynamic-slice_fusion.9
  13.5 0.6 reduce-window.25
  15.1 0.7 fusion.73
  15.8 1.0 fusion.72
  16.9 1.3 constant_dynamic-slice_fusion.8
  18.7 4.7 bitcast_dynamic-update-slice_fusion.2
  24.8 0.6 compare_convert_fusion.5
  25.6 0.9 bitcast_convert_fusion.2
  26.4 1.4 fusion.74
  28.0 0.8 multiply_dynamic-update-slice_fusion.2
  29.2 0.9 constant_dynamic-slice_fusion.9
  31.6 0.7 fusion.73
  32.3 1.1 fusion.72
  33.4 1.3 constant_dynamic-slice_fusion.8
  35.2 4.8 bitcast_dynamic-update-slice_fusion.2
  41.4 0.6 compare_convert_fusion.5
  42.1 0.9 bitcast_convert_fusion.2
  43.0 1.4 fusion.74
  44.6 0.8 multiply_dynamic-update-slice_fusion.2
  45.8 2.7 slice_add_fusion
  48.6 0.7 all-gather.9.cloned.1.call-update
  49.3 0.7 all-gather.11.cloned.1.call-update
  51.2 23.3 %all-gather = f32[16,1,32]{2,1,0:T(1,128)S(1)} all-gather(f32[1,1,32]{2,1,0:T(1,128)S(1)} %get-tuple-element.196), channel_id=1, replica_groups=mesh['ctx'=16,'head'=2] {'ctx'}, dimensions={0}, use_global_device_ids=true | all-gather | bytes 2176 | tf_op jit(solution)/shard_map/all_gather | solution.py:17
  74.5 103.8 %all-gather.7.cloned.1.call-done = f32[16,32,128,64]{2,3,1,0:T(8,128)} async-done(((f32[1,32,128,64]{2,3,1,0:T(8,128)}), f32[16,32,128,64]{2,3,1,0:T(8,128)}) %all-gather.7.cloned.1.call-update) | async-done | bytes 16777232 | tf_op jit(solution)/shard_map/all_gather | solution.py:17
  178.3 1.5 broadcast.134
  179.9 2.3 copy.51
  182.3 2.2 fusion.28
  184.5 1.2 copy-done.4
  185.7 1.4 fusion.27
  187.1 2.5 pad_maximum_fusion
  189.6 5.5 %copy.52 = f32[512,2048]{1,0:T(8,128)} copy(f32[512,2048]{0,1:T(8,128)} %bitcast.130) | data formatting | bytes 8388608 | tf_op jit(solution)/shard_map/reshape | solution.py:113
  195.1 3.6 multiply_reduce_fusion.1
  198.7 5.1 psum.14
  203.8 49.8 %all-gather.9.cloned.1.call-done = bf16[2048,2048]{1,0:T(8,128)(2,1)} async-done(((bf16[128,2048]{1,0:T(8,128)(2,1)}), bf16[2048,2048]{1,0:T(8,128)(2,1)}) %all-gather.9.cloned.1.call-update) | async-done | bytes 8388624 | tf_op jit(solution)/shard_map/all_gather | solution.py:121
  253.6 11.6 %fusion.26 = f32[512,2048]{1,0:T(8,128)} fusion(bf16[2048,2048]{1,0:T(8,128)(2,1)} %all-gather.9.cloned.1.call-done, f32[2048]{0:T(1024)S(1)} %copy-done.8, f32[512]{0:T(512)S(1)} %add_rsqrt_fusion.1, f32[512,2048]{1,0:T(8,128)} %copy.52, bf16[512,2048]{1,0:T(8,128)(2,1)S(1)} %copy-done.5), kind=kOutput, calls=%fused_computation.59 | convolution fusion | flops 4304404480 | bytes 18884608 | tf_op jit(solution)/shard_map/dot_general | solution.py:119
  265.2 3.4 add_dynamic-update-slice_fusion
  268.6 101.7 %all-reduce.1 = bf16[512,2048]{1,0:T(8,128)(2,1)S(1)} all-reduce(f32[512,2048]{1,0:T(8,128)} %add_dynamic-update-slice_fusion), channel_id=1, replica_groups=mesh['ctx'=16,'head'=2] {'head'}, use_global_device_ids=true, to_apply=%region_10.11 | all-reduce | flops 1048576 | bytes 6291456 | tf_op jit(solution)/shard_map/psum | solution.py:129
  370.8 9.6 %fusion.35 = f32[512,2048]{1,0:T(8,128)} fusion(bf16[2048,2048]{1,0:T(8,128)(2,1)} %all-gather.11.cloned.1.call-done, bf16[512,2048]{1,0:T(8,128)(2,1)S(1)} %all-reduce.1, f32[2048]{0:T(1024)S(1)} %copy-done.9, f32[512]{0:T(512)S(1)} %add_rsqrt_fusion), kind=kOutput, calls=%fused_computation.74 | convolution fusion | flops 4299161600 | bytes 14690304 | tf_op jit(solution)/shard_map/dot_general | solution.py:139
  380.5 23.7 %all-gather.13.cloned.1.call-done = bf16[2048,2048]{1,0:T(8,128)(2,1)} async-done(((bf16[128,2048]{1,0:T(8,128)(2,1)}), bf16[2048,2048]{1,0:T(8,128)(2,1)}) %all-gather.13.cloned.1.call-update) | async-done | bytes 8388624 | tf_op jit(solution)/shard_map/all_gather | solution.py:136
  404.2 75.2 %all-gather.15.cloned.1.call-done = bf16[2048,2048]{1,0:T(8,128)(2,1)} async-done(((bf16[128,2048]{1,0:T(8,128)(2,1)}), bf16[2048,2048]{1,0:T(8,128)(2,1)}) %all-gather.15.cloned.1.call-update) | async-done | bytes 8388624 | tf_op jit(solution)/shard_map/all_gather | solution.py:145
  479.4 17.5 %convolution_convert_fusion = bf16[512,2048]{1,0:T(8,128)(2,1)} fusion(bf16[2048,2048]{1,0:T(8,128)(2,1)} %all-gather.15.cloned.1.call-done, f32[512,2048]{1,0:T(8,128)} %fusion.35, bf16[2048,2048]{1,0:T(8,128)(2,1)} %all-gather.13.cloned.1.call-done, bf16[512,2048]{1,0:T(8,128)(2,1)S(1)} %all-reduce.1, f32[2048]{0:T(1024)S(1)} %copy-done.9, ...), kind=kOutput, calls=%fused_computation.58 | convolution fusion | flops 8601468928 | bytes 25176064 | tf_op jit(solution)/shard_map/dot_general | solution.py:143
  496.9 30.2 %reduce-scatter.2.cloned.1.call-done = bf16[512,1024]{1,0:T(8,128)(2,1)} async-done(((bf16[512,2048]{1,0:T(8,128)(2,1)}), bf16[512,1024]{1,0:T(8,128)(2,1)}) %reduce-scatter.2.cloned.1.call-update) | async-done | bytes 1048592 | tf_op jit(solution)/shard_map/reduce_scatter | solution.py:148
  527.2 2.5 multiply_convert_fusion.9
  (86 shorter events, 8.1 us)
Async XLA Ops:
  6.5 6.1 %copy-start.10 = (f32[32]{0:T(128)S(1)}, f32[32]{0:T(128)}, u32[]{:S(2)}) copy-start(f32[32]{0:T(128)} %param.26) | copy-start | bytes 388
  6.5 171.8 %all-gather.7.cloned.1.call-start = ((), (), s32[]{:S(2)}) async-start(), calls=%async_computation.1 | async-start | bytes 17825792 | tf_op jit(solution)/shard_map/all_gather | solution.py:17
  18.7 7.7 %copy-start.1 = (f32[2,32,128,64]{2,3,1,0:T(8,128)S(1)}, f32[2,32,128,64]{2,3,1,0:T(8,128)}, u32[]{:S(2)}) copy-start(f32[2,32,128,64]{2,3,1,0:T(8,128)} %get-tuple-element.324) | copy-start | bytes 6291460 | tf_op jit(solution)/shard_map/while
  27.9 1.3 copy-start.2
  35.2 7.7 %copy-start.1 = (f32[2,32,128,64]{2,3,1,0:T(8,128)S(1)}, f32[2,32,128,64]{2,3,1,0:T(8,128)}, u32[]{:S(2)}) copy-start(f32[2,32,128,64]{2,3,1,0:T(8,128)} %get-tuple-element.324) | copy-start | bytes 6291460 | tf_op jit(solution)/shard_map/while
  44.4 1.3 copy-start.2
  45.8 28.8 %copy-start.7 = (f32[2,32,256]{2,1,0:T(8,128)S(1)}, f32[2,32,256]{2,1,0:T(8,128)}, u32[]{:S(2)}) copy-start(f32[2,32,256]{2,1,0:T(8,128)} %get-tuple-element.113) | copy-start | bytes 196612
  48.5 205.1 %all-gather.9.cloned.1.call-start = ((), (), s32[]{:S(2)}) async-start(), calls=%async_computation.2 | async-start | bytes 8912896 | tf_op jit(solution)/shard_map/all_gather | solution.py:121
  49.3 321.5 %all-gather.11.cloned.1.call-start = ((), (), s32[]{:S(2)}) async-start(), calls=%async_computation.3 | async-start | bytes 8912896 | tf_op jit(solution)/shard_map/all_gather | solution.py:135
  50.0 354.1 %all-gather.13.cloned.1.call-start = ((), (), s32[]{:S(2)}) async-start(), calls=%async_computation.4 | async-start | bytes 8912896 | tf_op jit(solution)/shard_map/all_gather | solution.py:136
  50.6 428.7 %all-gather.15.cloned.1.call-start = ((), (), s32[]{:S(2)}) async-start(), calls=%async_computation.5 | async-start | bytes 8912896 | tf_op jit(solution)/shard_map/all_gather | solution.py:145
  51.2 476.0 %reduce-scatter.2.cloned.1.call-start = ((), (), s32[]{:S(2)}) async-start(), calls=%async_computation.6 | async-start | bytes 3145728 | tf_op jit(solution)/shard_map/reduce_scatter | solution.py:148
  179.9 2.4 copy-start
  182.2 2.3 copy-start.3
  182.2 3.5 copy-start.4
  189.6 5.5 %copy-start.5 = (bf16[512,2048]{1,0:T(8,128)(2,1)S(1)}, bf16[512,2048]{1,0:T(8,128)(2,1)}, u32[]{:S(2)}) copy-start(bf16[512,2048]{1,0:T(8,128)(2,1)} %param.20) | copy-start | bytes 6291460
  195.1 58.5 %copy-start.8 = (f32[2048]{0:T(1024)S(1)}, f32[2048]{0:T(1024)}, u32[]{:S(2)}) copy-start(f32[2048]{0:T(1024)} %param.27) | copy-start | bytes 24580
  203.8 61.4 %copy-start.6 = (bf16[512,1024]{1,0:T(8,128)(2,1)S(1)}, bf16[512,1024]{1,0:T(8,128)(2,1)}, u32[]{:S(2)}) copy-start(bf16[512,1024]{1,0:T(8,128)(2,1)} %param.28) | copy-start | bytes 3145732
  268.6 102.2 %copy-start.9 = (f32[2048]{0:T(1024)S(1)}, f32[2048]{0:T(1024)}, u32[]{:S(2)}) copy-start(f32[2048]{0:T(1024)} %param.30) | copy-start | bytes 24580
Sparse Core Ops, SparseCore 0:
  48.7 129.6 all-gather.6
  180.5 73.0 all-gather.8
  255.8 73.1 all-gather.10
  331.0 73.1 all-gather.12
  406.2 73.1 all-gather.14
  497.0 30.0 reduce-scatter.1
where the time goes:
time: 539 us; the launch traced here: 537 us
  waiting for transfers between devices  285 us (53%)
  blocking collectives  130 us (24%)
  matrix products  56.9 us (11%)
  other arithmetic  28 us (5%)
  local copies, waits for them, and re-layouts  21.2 us (4%)
  between operations  13.6 us (3%)
    all_gather x1, waiting for transfers between devices, carried_in(): gathered = jax.tree.map(lambda a: lax.all_gather(a, axis), part)  104 us
    psum x1, blocking collectives, shards(): hidden_full = lax.psum(projected + placed, 'head').astype(jnp.bfloat16)  102 us
    all_gather x1, waiting for transfers between devices, shards(): lax.all_gather(down_weight, 'ctx', axis=0, tiled=True)  75.2 us
    all_gather x1, waiting for transfers between devices, shards(): lax.all_gather(out_weight, 'ctx', axis=0, tiled=True)  49.8 us
    reduce_scatter x1, waiting for transfers between devices, shards(): lax.psum_scatter(down_out.astype(jnp.bfloat16), 'head', scatter_dimension...  30.2 us
    all_gather x1, waiting for transfers between devices, shards(): lax.all_gather(up_weight, 'ctx', axis=0, tiled=True)  23.7 us
    all_gather x1, blocking collectives, carried_in(): gathered = jax.tree.map(lambda a: lax.all_gather(a, axis), part)  23.3 us
    dot_general x1, matrix products, shards(): jnp.dot(columns, lax.all_gather(down_weight, 'ctx', axis=0, tiled=True),...  17.5 us
  transfers between devices with their start and end apart: 6, of which 5 were waited for; matrix products, arithmetic and copies ran while one was open for 8% of the time, Pallas kernels for 0%

commit v1 on v0

v1 whole, which is shorter than its diff:
```python
import functools

import jax
import jax.numpy as jnp
from jax import lax
from jax.experimental import pallas as pl
from jax.experimental.pallas import tpu as pltpu
from jax.sharding import PartitionSpec as P

HDIM = 64
STATE = 128
GROUP = 256
INNER = 4096
TILE = 256
LANES = 128

EPS = 1e-05
MESH = pl.DeviceIdType.MESH


def carried_in(factor, state):
    n = lax.axis_size("ctx")
    place = lax.axis_index("ctx")
    heads = state.shape[0]
    rows = heads * HDIM // n
    blocks = state.astype(jnp.bfloat16).reshape(n, rows, STATE)
    coarse = factor.astype(jnp.bfloat16)
    fine = (factor - coarse.astype(jnp.float32)).astype(jnp.bfloat16)
    tail = jnp.pad(jnp.stack([coarse, fine]), ((0, 14), (0, LANES - heads)))
    packed = jnp.concatenate([blocks, jnp.broadcast_to(tail[None], (n, 16, LANES))], axis=1)
    packed = lax.all_to_all(packed, "ctx", 0, 0)
    factors = packed[:, rows, :heads].astype(jnp.float32) + packed[:, rows + 1, :heads].astype(
        jnp.float32
    )
    owner = (place * rows + jnp.arange(rows)) // HDIM
    row_factors = jnp.take(factors, owner, axis=1)
    run = jnp.zeros((rows, STATE), jnp.float32)
    entering = []
    for source in range(n):
        entering.append(run.astype(jnp.bfloat16))
        run = row_factors[source][:, None] * run + packed[source, :rows].astype(jnp.float32)
    back = lax.all_to_all(jnp.stack(entering), "ctx", 0, 0)
    return back.reshape(heads, HDIM, STATE).astype(jnp.float32)


def group_core(masked, write_group, read_group, log_group, start_group, skip_gain):
    positions = jnp.arange(GROUP)
    log_sums = jnp.cumsum(log_group, axis=1)
    doc_index = jnp.cumsum(start_group)
    same_doc = (doc_index[:, None] == doc_index[None, :]) & (
        positions[:, None] >= positions[None, :]
    )
    scores = jnp.dot(read_group, write_group.T, preferred_element_type=jnp.float32)
    log_gaps = jnp.where(same_doc[None], log_sums[:, :, None] - log_sums[:, None, :], 0.0)
    weights = jnp.where(same_doc[None], scores[None] * jnp.exp(log_gaps), 0.0).astype(jnp.bfloat16)
    per_head = masked.reshape(GROUP, -1, HDIM)
    intra_out = jnp.einsum("hij,jhp->ihp", weights, per_head, preferred_element_type=jnp.float32)
    tail_wts = (
        jnp.exp(log_sums[:, -1:] - log_sums)
        * (doc_index == doc_index[-1]).astype(jnp.float32)[None]
    )
    weighted = (write_group.astype(jnp.float32)[None] * tail_wts[:, :, None]).astype(jnp.bfloat16)
    local_state = jnp.einsum("hjn,jhp->hpn", weighted, per_head, preferred_element_type=jnp.float32)
    reach_wts = jnp.exp(log_sums) * (doc_index == 0).astype(jnp.float32)[None]
    decay_all = jnp.exp(log_sums[:, -1]) * (doc_index[-1] == 0).astype(jnp.float32)
    direct = intra_out + skip_gain[None, :, None] * per_head.astype(jnp.float32)
    return (direct, local_state, reach_wts, decay_all)


def block_kernel(
    n, peers, normed, res, wout, g_sh, u_sh, d_sh, gain, live, out,
    wg, wu, wd, psend, precv, own, hid, scaled, act, dsend, drecv,
    ring_s, ring_r, x_s, x_r, sib_s, sib_r, y_s, y_r,
):
    me, y = lax.axis_index("ctx"), lax.axis_index("head")
    c, b, a = me % 2, (me // 2) % 2, me // 4
    ring = n // 4
    half = res.shape[1]
    toks = res.shape[0]
    sib = (me + 1 - 2 * c, y)
    across = (me + 2 - 4 * b, y)
    after = (((a + 1) % ring) * 4 + b * 2 + c, y)
    before = (((a + ring - 1) % ring) * 4 + b * 2 + c, y)
    others = [lax.rem(y + j, peers) for j in range(1, peers)]
    mine = pl.multiple_of(y * half, half)
    starts = [pl.multiple_of(other * half, half) for other in others] + [mine]

    barrier = pltpu.get_barrier_semaphore()
    for device in [sib, across, after, before] + [(me, other) for other in others]:
        pl.semaphore_signal(barrier, inc=1, device_id=device, device_id_type=MESH)
    pl.semaphore_wait(barrier, 3 + peers)

    full = [wg, wu] + [wd.at[j] for j in range(peers)]
    shard = [g_sh, u_sh] + [d_sh.at[:, pl.ds(start, half)] for start in starts]
    parts = len(full)

    def rows(p, k, bb, cc):
        slot = ((a + ring - k) % ring) * 4 + bb * 2 + cc
        depth = shard[p].shape[0]
        return pl.ds(pl.multiple_of(slot * depth, depth), depth)

    def remote(src, dst, send, recv, device):
        return pltpu.make_async_remote_copy(
            src_ref=src, dst_ref=dst, send_sem=send, recv_sem=recv,
            device_id=device, device_id_type=MESH,
        )

    def column(p, k):
        place = full[p].at[rows(p, k, b, c)]
        return (shard[p] if k == 0 else place), place

    def ring_copy(p, k):
        src, dst = column(p, k)
        return remote(src, dst, ring_s.at[p, k], ring_r.at[p, k], after)

    def x_copy(p, k):
        src, dst = column(p, k)
        return remote(src, dst, x_s.at[p, k], x_r.at[p, k], across)

    def sib_copy(p, k):
        if k < ring:
            src, dst = column(p, k)
        else:
            src = dst = full[p].at[rows(p, k - ring, 1 - b, c)]
        return remote(src, dst, sib_s.at[p, k], sib_r.at[p, k], sib)

    def spread(p, k):
        if k < ring - 1:
            ring_copy(p, k).start()
        x_copy(p, k).start()
        sib_copy(p, k).start()

    def begin(p):
        spread(p, 0)
        full[p][rows(p, 0, b, c), :] = shard[p][...]

    def ring_step(p, k):
        place = full[p].at[rows(p, k, b, c)]
        remote(place, place, ring_s.at[p, k - 1], ring_r.at[p, k - 1], after).wait_recv()
        spread(p, k)

    def ring_steps(p):
        for k in range(1, ring):
            ring_step(p, k)

    def x_steps(p):
        for k in range(ring):
            place = full[p].at[rows(p, k, 1 - b, c)]
            remote(place, place, x_s.at[p, k], x_r.at[p, k], across).wait_recv()
            sib_copy(p, ring + k).start()

    def finish(p):
        for k in range(2 * ring):
            bb = b if k < ring else 1 - b
            place = full[p].at[rows(p, k % ring, bb, 1 - c)]
            remote(place, place, sib_s.at[p, k], sib_r.at[p, k], sib).wait_recv()

    begin(0)
    begin(1)

    def y_copy(stage, j, src, dst):
        return remote(src, dst, y_s.at[stage, j], y_r.at[stage, j], (me, others[j]))

    part_copies = [y_copy(0, j, psend.at[j], precv.at[j]) for j in range(peers - 1)]
    for j in range(peers - 1):

        @pl.loop(0, half // TILE)
        def _(t):
            src = pl.ds(pl.multiple_of(starts[j] + t * TILE, TILE), TILE)
            dst = pl.ds(pl.multiple_of(t * TILE, TILE), TILE)
            psend[j, :, dst] = jnp.dot(
                normed[...], wout[:, src], preferred_element_type=jnp.float32
            ).astype(jnp.bfloat16)

        part_copies[j].start()
    ring_step(0, 1)

    @pl.loop(0, half // TILE)
    def _(t):
        src = pl.ds(pl.multiple_of(mine + t * TILE, TILE), TILE)
        dst = pl.ds(pl.multiple_of(t * TILE, TILE), TILE)
        own[:, dst] = res[:, dst].astype(jnp.float32) + jnp.dot(
            normed[...], wout[:, src], preferred_element_type=jnp.float32
        )

    for k in range(2, ring):
        ring_step(0, k)
    begin(2)
    for copy in part_copies:
        copy.wait_recv()

    @pl.loop(0, half // TILE)
    def _(t):
        src = pl.ds(pl.multiple_of(t * TILE, TILE), TILE)
        dst = pl.ds(pl.multiple_of(mine + t * TILE, TILE), TILE)
        total = own[:, src]
        for j in range(peers - 1):
            total += precv[j, :, src].astype(jnp.float32)
        hid[:, dst] = total.astype(jnp.bfloat16)

    kept = hid.at[:, pl.ds(mine, half)]
    hid_copies = [y_copy(1, j, kept, kept) for j in range(peers - 1)]
    for copy in hid_copies:
        copy.start()
    x_steps(0)
    ring_steps(1)
    begin(3)
    for j in range(peers - 1):
        sender = lax.rem(y + peers - 1 - j, peers)
        place = hid.at[:, pl.ds(pl.multiple_of(sender * half, half), half)]
        y_copy(1, j, place, place).wait_recv()

    @pl.loop(0, toks // 64)
    def _(t):
        part = pl.ds(pl.multiple_of(t * 64, 64), 64)
        wide = hid[part, :].astype(jnp.float32)
        scale = lax.rsqrt(jnp.mean(wide * wide, axis=1, keepdims=True) + EPS)
        scaled[part, :] = (wide * scale * gain[...]).astype(jnp.bfloat16)

    x_steps(1)
    ring_step(2, 1)
    finish(0)
    finish(1)
    for k in range(2, ring):
        ring_step(2, k)
    ring_step(3, 1)

    @pl.loop(0, wg.shape[1] // TILE)
    def _(t):
        cols = pl.ds(pl.multiple_of(t * TILE, TILE), TILE)
        gate = jnp.dot(scaled[...], wg[:, cols], preferred_element_type=jnp.float32)
        up = jnp.dot(scaled[...], wu[:, cols], preferred_element_type=jnp.float32)
        act[:, cols] = (jax.nn.silu(gate) * up).astype(jnp.bfloat16)

    down_copies = [y_copy(2, j, dsend.at[j], drecv.at[j]) for j in range(peers - 1)]
    for j in range(peers - 1):
        p = 2 + j
        x_steps(p)
        for k in range(2, ring):
            ring_step(p + 1, k)
        if p + 2 < parts:
            begin(p + 2)
            ring_step(p + 2, 1)
        finish(p)

        @pl.loop(0, half // TILE)
        def _(t):
            cols = pl.ds(pl.multiple_of(t * TILE, TILE), TILE)
            dsend[j, :, cols] = jnp.dot(
                act[...], wd[j, :, cols], preferred_element_type=jnp.float32
            ).astype(jnp.bfloat16)

        down_copies[j].start()
    x_steps(parts - 1)
    finish(parts - 1)

    @pl.loop(0, half // TILE)
    def _(t):
        cols = pl.ds(pl.multiple_of(t * TILE, TILE), TILE)
        kept = pl.ds(pl.multiple_of(mine + t * TILE, TILE), TILE)
        own[:, cols] = hid[:, kept].astype(jnp.float32) + jnp.dot(
            act[...], wd[peers - 1, :, cols], preferred_element_type=jnp.float32
        )

    for copy in down_copies:
        copy.wait_recv()

    @pl.loop(0, half // TILE)
    def _(t):
        cols = pl.ds(pl.multiple_of(t * TILE, TILE), TILE)
        total = own[:, cols]
        for j in range(peers - 1):
            total += drecv[j, :, cols].astype(jnp.float32)
        out[:, cols] = (live[...] * total).astype(jnp.bfloat16)

    for copy in part_copies + hid_copies + down_copies:
        copy.wait_send()
    for p in range(parts):
        for k in range(ring):
            if k < ring - 1:
                ring_copy(p, k).wait_send()
            x_copy(p, k).wait_send()
        for k in range(2 * ring):
            sib_copy(p, k).wait_send()


def block(normed, residual, wout, gate_weight, up_weight, down_weight, mlp_gain, live):
    n, peers = lax.axis_size("ctx"), lax.axis_size("head")
    ring, parts = n // 4, 2 + peers
    toks, half = residual.shape
    width = wout.shape[1]
    deep = gate_weight.shape[0] * n
    units = gate_weight.shape[1]
    bf, f32 = jnp.bfloat16, jnp.float32
    sems = pltpu.SemaphoreType.DMA
    return pl.pallas_call(
        functools.partial(block_kernel, n, peers),
        out_shape=jax.ShapeDtypeStruct((toks, half), bf),
        in_specs=[pl.BlockSpec(memory_space=pltpu.VMEM)] * 8,
        out_specs=pl.BlockSpec(memory_space=pltpu.VMEM),
        scratch_shapes=[
            pltpu.VMEM((deep, units), bf),
            pltpu.VMEM((deep, units), bf),
            pltpu.VMEM((peers, units, half), bf),
            pltpu.VMEM((peers - 1, toks, half), bf),
            pltpu.VMEM((peers - 1, toks, half), bf),
            pltpu.VMEM((toks, half), f32),
            pltpu.VMEM((toks, width), bf),
            pltpu.VMEM((toks, width), bf),
            pltpu.VMEM((toks, units), bf),
            pltpu.VMEM((peers - 1, toks, half), bf),
            pltpu.VMEM((peers - 1, toks, half), bf),
            sems((parts, ring)), sems((parts, ring)),
            sems((parts, ring)), sems((parts, ring)),
            sems((parts, 2 * ring)), sems((parts, 2 * ring)),
            sems((3, peers - 1)), sems((3, peers - 1)),
        ],
        compiler_params=pltpu.CompilerParams(
            collective_id=0, has_side_effects=True, vmem_limit_bytes=60 * 1024 * 1024
        ),
        cost_estimate=pl.CostEstimate(
            flops=2 * toks * (2048 * width + 3 * deep * units),
            bytes_accessed=40 * 1024 * 1024,
            transcendentals=toks * units,
        ),
    )(normed, residual, wout, gate_weight, up_weight, down_weight, mlp_gain, live)


def shards(
    mixer_input,
    gate_input,
    write_vecs,
    read_vecs,
    log_decay,
    doc_start,
    live_mask,
    skip_gain,
    norm_gain,
    residual,
    out_weight,
    mlp_gain,
    gate_weight,
    up_weight,
    down_weight,
):
    tok_rows = mixer_input.shape[0]
    group_total = tok_rows // GROUP
    head_count = log_decay.shape[0]
    wout = lax.all_gather(out_weight, "ctx", axis=0, tiled=True)
    masked = mixer_input * live_mask.astype(jnp.bfloat16)[:, None]
    read_groups = read_vecs.reshape(group_total, GROUP, -1)
    group_data = (
        masked.reshape(group_total, GROUP, -1),
        write_vecs.reshape(group_total, GROUP, -1),
        read_groups,
        log_decay.reshape(head_count, group_total, GROUP).transpose(1, 0, 2),
        doc_start.reshape(group_total, GROUP),
    )

    def group_step(pieces):
        return group_core(pieces[0], pieces[1], pieces[2], pieces[3], pieces[4], skip_gain)

    directs, local_parts, reaches, decays = lax.map(group_step, group_data)
    run_state = jnp.zeros((head_count, HDIM, STATE), jnp.float32)
    run_factor = jnp.ones((head_count,), jnp.float32)
    before = []
    factors = []
    for group_id in range(group_total):
        before.append(run_state)
        factors.append(run_factor)
        run_state = decays[group_id][:, None, None] * run_state + local_parts[group_id]
        run_factor = run_factor * decays[group_id]
    incoming = carried_in(run_factor, run_state)
    outputs = []
    for group_id in range(group_total):
        inner_state = (factors[group_id][:, None, None] * incoming + before[group_id]).astype(
            jnp.bfloat16
        )
        crossed = jnp.einsum(
            "in,hpn->ihp", read_groups[group_id], inner_state, preferred_element_type=jnp.float32
        )
        outputs.append(directs[group_id] + crossed * reaches[group_id].T[:, :, None])
    output = jnp.concatenate(outputs, axis=0).reshape(tok_rows, -1)
    gated = output * jax.nn.silu(gate_input.astype(jnp.float32))
    squares = lax.psum(jnp.sum(gated * gated, axis=1), "head")
    normed = (gated * lax.rsqrt(squares / INNER + EPS)[:, None] * norm_gain).astype(jnp.bfloat16)
    return block(
        normed,
        residual,
        wout,
        gate_weight,
        up_weight,
        down_weight,
        mlp_gain[None, :],
        live_mask.astype(jnp.float32)[:, None],
    )


def solution(mesh):
    return jax.shard_map(
        shards,
        mesh=mesh,
        in_specs=(
            P("ctx", "head"),
            P("ctx", "head"),
            P("ctx", None),
            P("ctx", None),
            P("head", "ctx"),
            P("ctx"),
            P("ctx"),
            P("head"),
            P("head"),
            P("ctx", "head"),
            P(("head", "ctx"), None),
            P(),
            P("ctx", "head"),
            P("ctx", "head"),
            P(("head", "ctx"), None),
        ),
        out_specs=P("ctx", "head"),
        check_vma=False,
    )
```

time: 539 us -> 312 us (0.58)
  waiting for transfers between devices: 285 us -> 38.6 us
  Pallas kernels: 0 us -> 166 us
  blocking collectives: 130 us -> 5.12 us
  matrix products: 56.9 us -> 15.6 us
  starting transfers between devices: 0.2 us -> 18.2 us
    all_gather x5 -> x1, waiting for transfers between devices: 252 us -> 0.01 us  [shards(): wout = lax.all_gather(out_weight, 'ctx', axis=0, tiled=True)]
    pallas_call x0 -> x1, Pallas kernels: none -> 166 us  [block(): pl.pallas_call(functools.partial(block_kernel, n, peers), out_shape=jax.S...]
    psum x1 -> x0, blocking collectives: 102 us -> none  [shards(): hidden_full = lax.psum(projected + placed, 'head').astype(jnp.bfloat16)]
    all_to_all x0 -> x2, waiting for transfers between devices: none -> 37.9 us  [the longest x1 24.5 us: carried_in(): packed = lax.all_to_all(packed, 'ctx', 0, 0)]
    dot_general x7 -> x4, matrix products: 45.3 us -> 7.64 us  [the longest x2 4.89 us: group_core(): jnp.einsum('hjn,jhp->hpn', weighted, per_head, preferred_element_type=jnp...]
    reduce_scatter x1 -> x0, waiting for transfers between devices: 30.2 us -> none  [shards(): lax.psum_scatter(down_out.astype(jnp.bfloat16), 'head', scatter_dimension...]
    all_gather x1 -> x0, blocking collectives: 23.3 us -> none  [carried_in(): gathered = jax.tree.map(lambda a: lax.all_gather(a, axis), part)]
    all_to_all x0 -> x2, starting transfers between devices: none -> 18.2 us  [the longest x1 10.8 us: carried_in(): back = lax.all_to_all(jnp.stack(entering), 'ctx', 0, 0)]
  transfers between devices with their start and end apart: 6 -> 3, of which waited for: 5 -> 2; matrix products, arithmetic and copies ran while one was open for 8% -> 21% of each run, Pallas kernels for 0% -> 0%
where the time goes in v1:
time: 312 us; the launch traced here: 311 us
  Pallas kernels  166 us (53%)
  waiting for transfers between devices  38.6 us (12%)
  other arithmetic  32.9 us (11%)
  local copies, waits for them, and re-layouts  19.9 us (6%)
  starting transfers between devices  18.2 us (6%)
  matrix products  15.6 us (5%)
  between operations  13.6 us (4%)
  blocking collectives  5.12 us (2%)
    pallas_call x1, Pallas kernels, block(): pl.pallas_call(functools.partial(block_kernel, n, peers), out_shape=jax.S...  166 us
    all_to_all x1, waiting for transfers between devices, carried_in(): packed = lax.all_to_all(packed, 'ctx', 0, 0)  24.5 us
    all_to_all x1, waiting for transfers between devices, carried_in(): back = lax.all_to_all(jnp.stack(entering), 'ctx', 0, 0)  13.4 us
    all_to_all x1, starting transfers between devices, carried_in(): back = lax.all_to_all(jnp.stack(entering), 'ctx', 0, 0)  10.8 us
    unnamed x14, other arithmetic  9.88 us
    dot_general x2, matrix products, group_core(): jnp.einsum('hij,jhp->ihp', weights, per_head, preferred_element_type=jnp....  7.58 us
    all_to_all x1, starting transfers between devices, carried_in(): packed = lax.all_to_all(packed, 'ctx', 0, 0)  7.38 us
  transfers between devices with their start and end apart: 3, of which 2 were waited for; matrix products, arithmetic and copies ran while one was open for 21% of the time, Pallas kernels for 0%

profile of v1, /device:TPU:0, one launch (start us, length us, event | category | flops | bytes accessed | tf_op | source)
XLA Modules:
  0.0 311.1 jit_solution(7594747320052541956)
XLA Ops:
  6.5 0.7 all-gather.2.cloned.1.call-update
  7.3 0.8 fusion.57
  8.1 0.9 reshape.1068
  8.9 0.7 reshape.1065
  9.6 3.2 %broadcast_multiply_fusion = bf16[512,2048]{1,0:T(8,128)(2,1)} fusion(bf16[512,2048]{1,0:T(8,128)(2,1)} %param.17, bf16[512]{0:T(512)(128)(2,1)S(1)} %get-tuple-element.164), kind=kLoop, calls=%fused_computation.56 | loop fusion | flops 1048576 | bytes 4195328 | tf_op jit(solution)/shard_map/mul | solution.py:350
  12.8 24.3 %while.16 = (s32[]{:T(128)}, f32[2,256,32,64]{1,3,2,0:T(8,128)}, f32[2,32,64,128]{3,2,1,0:T(8,128)}, f32[2,32,256]{2,1,0:T(8,128)S(1)}, f32[2,32]{1,0:T(2,128)S(...) while((s32[]{:T(128)}, f32[2,256,32,64]{1,3,2,0:T(8,128)}, ...), condition=%wide.region_5.6_spmd, body=%wide.region_0.5_spmd.sunk | while | flops 434922624 | bytes 12338567 | solution.py:363
  12.9 0.6 reduce-window.25
  14.7 1.3 constant_dynamic-slice_fusion.6
  16.6 3.8 %bitcast_dynamic-update-slice_fusion.2 = f32[2,256,32,64]{1,3,2,0:T(8,128)} fusion(f32[2,256,32,64]{1,3,2,0:T(8,128)} %get-tuple-element.261, s32[]{:T(128)} %get-tuple-element.260, bf16[256,32,64]{0,2,1:T(8,128)(2,1)S(1)} %bitcast.109, f32[32,256]{1,0:T(8,128)S(1)} %bitcast.119, f32[256,256]{1,0:T(8,128)S(1)} %fusion.73, ...), kind=kOutput, calls=%fused_computation.10.clone.1 | convolution fusion | flops 280494080 | bytes 4588544 | tf_op jit(solution)/shard_map/while/body/eval_jaxpr/hij,jhp->ihp/dot_general | solution.py:57
  22.4 2.5 fusion.75
  26.9 1.3 constant_dynamic-slice_fusion.6
  28.7 3.8 %bitcast_dynamic-update-slice_fusion.2 = f32[2,256,32,64]{1,3,2,0:T(8,128)} fusion(f32[2,256,32,64]{1,3,2,0:T(8,128)} %get-tuple-element.261, s32[]{:T(128)} %get-tuple-element.260, bf16[256,32,64]{0,2,1:T(8,128)(2,1)S(1)} %bitcast.109, f32[32,256]{1,0:T(8,128)S(1)} %bitcast.119, f32[256,256]{1,0:T(8,128)S(1)} %fusion.73, ...), kind=kOutput, calls=%fused_computation.10.clone.1 | convolution fusion | flops 280494080 | bytes 4588544 | tf_op jit(solution)/shard_map/while/body/eval_jaxpr/hij,jhp->ihp/dot_general | solution.py:57
  34.5 2.4 fusion.75
  37.6 1.7 fusion.55
  39.3 0.6 add_convert_fusion.1
  40.0 0.9 pad_maximum_fusion.1
  40.8 7.4 %all-to-all-start = ((bf16[16,144,128]{2,1,0:T(8,128)(2,1)}), bf16[16,144,128]{2,1,0:T(8,128)(2,1)S(1)}, u32[]{:S(2)}, u32[]{:S(2)}) async-start(bf16[16,144,128]{2,1,0:T(8,128)(2,1)} %pad_maximum_fusion.1), calls=%async_computation | async-start | bytes 1179648 | tf_op jit(solution)/shard_map/all_to_all | solution.py:31
  48.3 0.6 constant_dynamic-update-slice_fusion.6
  48.9 24.5 %all-to-all-done = bf16[16,144,128]{2,1,0:T(8,128)(2,1)S(1)} async-done(((bf16[16,144,128]{2,1,0:T(8,128)(2,1)}), bf16[16,144,128]{2,1,0:T(8,128)(2,1)S(1)}, u32[]{:S(2)}, u32[]{:S(2)}) %all-to-all-start) | async-done | bytes 589856 | tf_op jit(solution)/shard_map/all_to_all | solution.py:31
  73.5 0.7 gather_fusion
  74.3 0.6 slice_reduce_fusion.3
  74.9 0.7 fusion.45
  75.6 0.7 fusion.44
  76.3 0.7 constant_dynamic-update-slice_fusion.5
  77.0 0.7 fusion.43
  77.7 0.8 constant_dynamic-update-slice_fusion.4
  78.5 0.7 fusion.42
  79.2 0.7 constant_dynamic-update-slice_fusion.3
  79.9 0.7 fusion.41
  80.6 0.7 constant_dynamic-update-slice_fusion.2
  81.3 0.7 fusion.40
  82.0 0.7 constant_dynamic-update-slice_fusion.1
  82.7 0.7 fusion.39
  83.4 0.7 constant_dynamic-update-slice_fusion
  84.1 0.7 fusion.38
  84.8 0.7 fusion.46
  85.5 10.8 %all-to-all-start.1 = ((bf16[16,128,128]{2,1,0:T(8,128)(2,1)}), bf16[16,128,128]{2,1,0:T(8,128)(2,1)S(1)}, u32[]{:S(2)}, u32[]{:S(2)}) async-start(bf16[16,128,128]{2,1,0:T(8,128)(2,1)} %fusion.46), calls=%async_computation.1 | async-start | bytes 1048576 | tf_op jit(solution)/shard_map/all_to_all | solution.py:42
  96.4 0.9 copy.60.live
  97.3 13.4 %all-to-all-done.1 = bf16[16,128,128]{2,1,0:T(8,128)(2,1)S(1)} async-done(((bf16[16,128,128]{2,1,0:T(8,128)(2,1)}), bf16[16,128,128]{2,1,0:T(8,128)(2,1)S(1)}, u32[]{:S(2)}, u32[]{:S(2)}) %all-to-all-start.1) | async-done | bytes 524320 | tf_op jit(solution)/shard_map/all_to_all | solution.py:42
  110.7 0.6 add_convert_fusion
  111.4 2.3 fusion.24
  114.1 2.5 pad_maximum_fusion
  116.6 5.6 %copy.59 = f32[512,2048]{1,0:T(8,128)} copy(f32[512,2048]{0,1:T(8,128)} %bitcast.111) | data formatting | bytes 8388608 | tf_op jit(solution)/shard_map/reshape | solution.py:383
  122.2 3.6 %multiply_reduce_fusion.1 = f32[512]{0:T(512)S(1)} fusion(f32[512,2048]{1,0:T(8,128)} %copy.59, bf16[512,2048]{1,0:T(8,128)(2,1)S(1)} %copy-done), kind=kLoop, calls=%fused_computation.49 | loop fusion | flops 8388096 | bytes 6293504 | tf_op jit(solution)/shard_map/reduce_sum | solution.py:385
  125.8 5.1 %psum.7 = f32[512]{0:T(512)S(1)} all-reduce(f32[512]{0:T(512)S(1)} %multiply_reduce_fusion.1), channel_id=1, replica_groups=mesh['ctx'=16,'head'=2] {'head'}, use_global_device_ids=true, to_apply=%region_7.8 | all-reduce | flops 512 | bytes 4096 | tf_op jit(solution)/shard_map/psum | solution.py:385
  130.9 5.2 %multiply_convert_fusion.6.normed = bf16[512,2048]{1,0:T(8,128)(2,1)} fusion(f32[2048]{0:T(1024)S(1)} %copy-done.4, f32[512]{0:T(512)S(1)} %add_rsqrt_fusion, f32[512,2048]{1,0:T(8,128)} %copy.59, bf16[512,2048]{1,0:T(8,128)(2,1)S(1)} %copy-done), kind=kLoop, calls=%fused_computation.48 | loop fusion | flops 9437184 | bytes 8398848 | tf_op jit(solution)/shard_map/convert_element_type | solution.py:386
  136.1 165.8 %shard_map.145 = bf16[512,1024]{1,0:T(8,128)(2,1)} custom-call(bf16[512,2048]{1,0:T(8,128)(2,1)} %multiply_convert_fusion.6.normed, bf16[512,1024]{1,0:T(8,128)(2,1)} %res.1, bf16[2048,2048]{1,0:T(8,128)(2,1)} %all-gather.2.cloned.1.call-done.wout, bf16[128,2048]{1,0:T(8,128)(2,1)} %g_sh.1, bf16[128,2048]{1,0:T(8,128)(2,1)} %u_sh.1, bf16[128,2048]{1,0:T(8,128)(2,1)} %d_sh.1, ...), custom_call_target="tpu_custom_call" | custom-call | flops 17179869184 | bytes 41943040 | tf_op jit(solution)/shard_map/pallas_call | solution.py:296
  302.0 2.3 copy.115
  (92 shorter events, 8.7 us)
Async XLA Ops:
  6.5 6.3 %copy-start.3 = (bf16[512,128]{1,0:T(8,128)(2,1)S(1)}, bf16[512,128]{1,0:T(8,128)(2,1)}, u32[]{:S(2)}) copy-start(bf16[512,128]{1,0:T(8,128)(2,1)} %param.20) | copy-start | bytes 393220
  6.5 6.3 %copy-start.2 = (bf16[512,128]{1,0:T(8,128)(2,1)S(1)}, bf16[512,128]{1,0:T(8,128)(2,1)}, u32[]{:S(2)}) copy-start(bf16[512,128]{1,0:T(8,128)(2,1)} %param.19) | copy-start | bytes 393220
  6.5 6.3 %copy-start.5 = (f32[32]{0:T(128)S(1)}, f32[32]{0:T(128)}, u32[]{:S(2)}) copy-start(f32[32]{0:T(128)} %param.24) | copy-start | bytes 388
  6.5 129.6 %all-gather.2.cloned.1.call-start = ((), (), s32[]{:S(2)}) async-start(), calls=%async_computation.2 | async-start | bytes 8912896 | tf_op jit(solution)/shard_map/all_gather | solution.py:349
  40.8 32.5 %all-to-all-start = ((bf16[16,144,128]{2,1,0:T(8,128)(2,1)}), bf16[16,144,128]{2,1,0:T(8,128)(2,1)S(1)}, u32[]{:S(2)}, u32[]{:S(2)}) async-start(bf16[16,144,128]{2,1,0:T(8,128)(2,1)} %pad_maximum_fusion.1), calls=%async_computation | async-start | bytes 1179648 | tf_op jit(solution)/shard_map/all_to_all | solution.py:31
  85.5 25.2 %all-to-all-start.1 = ((bf16[16,128,128]{2,1,0:T(8,128)(2,1)}), bf16[16,128,128]{2,1,0:T(8,128)(2,1)S(1)}, u32[]{:S(2)}, u32[]{:S(2)}) async-start(bf16[16,128,128]{2,1,0:T(8,128)(2,1)} %fusion.46), calls=%async_computation.1 | async-start | bytes 1048576 | tf_op jit(solution)/shard_map/all_to_all | solution.py:42
  110.7 2.9 copy-start.1
  116.6 5.6 %copy-start = (bf16[512,2048]{1,0:T(8,128)(2,1)S(1)}, bf16[512,2048]{1,0:T(8,128)(2,1)}, u32[]{:S(2)}) copy-start(bf16[512,2048]{1,0:T(8,128)(2,1)} %param.18) | copy-start | bytes 6291460
  122.2 8.7 %copy-start.4 = (f32[2048]{0:T(1024)S(1)}, f32[2048]{0:T(1024)}, u32[]{:S(2)}) copy-start(f32[2048]{0:T(1024)} %param.25) | copy-start | bytes 24580
Sparse Core Ops, SparseCore 0:
  9.5 87.8 all-gather.1

commit v2 on v1

--- a/solution.py
+++ b/solution.py
@@ -68,7 +68,7 @@
 
 
 def block_kernel(
-    n, peers, normed, res, wout, g_sh, u_sh, d_sh, gain, live, out,
+    n, peers, normed, res, wout, wga, g_sh, u_sh, d_sh, gain, live, out,
     wg, wu, wd, psend, precv, own, hid, scaled, act, dsend, drecv,
     ring_s, ring_r, x_s, x_r, sib_s, sib_r, y_s, y_r,
 ):
@@ -90,9 +90,11 @@
         pl.semaphore_signal(barrier, inc=1, device_id=device, device_id_type=MESH)
     pl.semaphore_wait(barrier, 3 + peers)
 
+    cut = wga.shape[1]
     full = [wg, wu] + [wd.at[j] for j in range(peers)]
-    shard = [g_sh, u_sh] + [d_sh.at[:, pl.ds(start, half)] for start in starts]
+    shard = [g_sh.at[:, pl.ds(cut, cut)], u_sh] + [d_sh.at[:, pl.ds(start, half)] for start in starts]
     parts = len(full)
+    swap_first = (2,)
 
     def rows(p, k, bb, cc):
         slot = ((a + ring - k) % ring) * 4 + bb * 2 + cc
@@ -109,8 +111,14 @@
         place = full[p].at[rows(p, k, b, c)]
         return (shard[p] if k == 0 else place), place
 
+    def sib_chunk(p, k):
+        if k < ring:
+            return column(p, k)
+        place = full[p].at[rows(p, k - ring, 1 - b, c)]
+        return place, place
+
     def ring_copy(p, k):
-        src, dst = column(p, k)
+        src, dst = sib_chunk(p, k)
         return remote(src, dst, ring_s.at[p, k], ring_r.at[p, k], after)
 
     def x_copy(p, k):
@@ -118,36 +126,44 @@
         return remote(src, dst, x_s.at[p, k], x_r.at[p, k], across)
 
     def sib_copy(p, k):
-        if k < ring:
-            src, dst = column(p, k)
-        else:
-            src = dst = full[p].at[rows(p, k - ring, 1 - b, c)]
+        src, dst = sib_chunk(p, k)
         return remote(src, dst, sib_s.at[p, k], sib_r.at[p, k], sib)
 
+    def swaps(p, k):
+        return p not in swap_first or k == 0
+
     def spread(p, k):
-        if k < ring - 1:
+        if k % ring < ring - 1:
             ring_copy(p, k).start()
-        x_copy(p, k).start()
+        if k < ring and swaps(p, k):
+            x_copy(p, k).start()
         sib_copy(p, k).start()
 
     def begin(p):
         spread(p, 0)
         full[p][rows(p, 0, b, c), :] = shard[p][...]
 
+    def x_wait(p, k):
+        place = full[p].at[rows(p, k, 1 - b, c)]
+        remote(place, place, x_s.at[p, k], x_r.at[p, k], across).wait_recv()
+
+    def swap(p):
+        x_wait(p, 0)
+        spread(p, ring)
+
     def ring_step(p, k):
-        place = full[p].at[rows(p, k, b, c)]
-        remote(place, place, ring_s.at[p, k - 1], ring_r.at[p, k - 1], after).wait_recv()
-        spread(p, k)
-
-    def ring_steps(p):
-        for k in range(1, ring):
-            ring_step(p, k)
+        for lane in (k, ring + k) if p in swap_first else (k,):
+            place = sib_chunk(p, lane)[1]
+            remote(
+                place, place, ring_s.at[p, lane - 1], ring_r.at[p, lane - 1], after
+            ).wait_recv()
+            spread(p, lane)
 
     def x_steps(p):
-        for k in range(ring):
-            place = full[p].at[rows(p, k, 1 - b, c)]
-            remote(place, place, x_s.at[p, k], x_r.at[p, k], across).wait_recv()
-            sib_copy(p, ring + k).start()
+        if p not in swap_first:
+            for k in range(ring):
+                x_wait(p, k)
+                sib_copy(p, ring + k).start()
 
     def finish(p):
         for k in range(2 * ring):
@@ -174,6 +190,7 @@
 
         part_copies[j].start()
     ring_step(0, 1)
+    begin(2)
 
     @pl.loop(0, half // TILE)
     def _(t):
@@ -183,9 +200,10 @@
             normed[...], wout[:, src], preferred_element_type=jnp.float32
         )
 
-    for k in range(2, ring):
+    ring_step(1, 1)
+    swap(2)
+    for k in range(2, ring - 1):
         ring_step(0, k)
-    begin(2)
     for copy in part_copies:
         copy.wait_recv()
 
@@ -202,9 +220,14 @@
     hid_copies = [y_copy(1, j, kept, kept) for j in range(peers - 1)]
     for copy in hid_copies:
         copy.start()
+    for k in range(2, ring - 1):
+        ring_step(1, k)
+    begin(3)
+    ring_step(0, ring - 1)
+    ring_step(1, ring - 1)
+    ring_step(2, 1)
+    ring_step(3, 1)
     x_steps(0)
-    ring_steps(1)
-    begin(3)
     for j in range(peers - 1):
         sender = lax.rem(y + peers - 1 - j, peers)
         place = hid.at[:, pl.ds(pl.multiple_of(sender * half, half), half)]
@@ -218,29 +241,34 @@
         scaled[part, :] = (wide * scale * gain[...]).astype(jnp.bfloat16)
 
     x_steps(1)
-    ring_step(2, 1)
+    for k in range(2, ring - 1):
+        ring_step(2, k)
+        ring_step(3, k)
     finish(0)
     finish(1)
-    for k in range(2, ring):
-        ring_step(2, k)
-    ring_step(3, 1)
-
-    @pl.loop(0, wg.shape[1] // TILE)
-    def _(t):
-        cols = pl.ds(pl.multiple_of(t * TILE, TILE), TILE)
-        gate = jnp.dot(scaled[...], wg[:, cols], preferred_element_type=jnp.float32)
-        up = jnp.dot(scaled[...], wu[:, cols], preferred_element_type=jnp.float32)
-        act[:, cols] = (jax.nn.silu(gate) * up).astype(jnp.bfloat16)
+
+    def gated_units(gate_ref, start):
+        @pl.loop(0, cut // TILE)
+        def _(t):
+            cols = pl.ds(pl.multiple_of(t * TILE, TILE), TILE)
+            wide = pl.ds(pl.multiple_of(start + t * TILE, TILE), TILE)
+            gate = jnp.dot(scaled[...], gate_ref[:, cols], preferred_element_type=jnp.float32)
+            up = jnp.dot(scaled[...], wu[:, wide], preferred_element_type=jnp.float32)
+            act[:, wide] = (jax.nn.silu(gate) * up).astype(jnp.bfloat16)
+
+    gated_units(wga, 0)
+    ring_step(2, ring - 1)
+    ring_step(3, ring - 1)
+    x_steps(2)
+    gated_units(wg, cut)
 
     down_copies = [y_copy(2, j, dsend.at[j], drecv.at[j]) for j in range(peers - 1)]
     for j in range(peers - 1):
         p = 2 + j
-        x_steps(p)
-        for k in range(2, ring):
-            ring_step(p + 1, k)
         if p + 2 < parts:
             begin(p + 2)
-            ring_step(p + 2, 1)
+        if j > 0:
+            x_steps(p)
         finish(p)
 
         @pl.loop(0, half // TILE)
@@ -251,6 +279,9 @@
             ).astype(jnp.bfloat16)
 
         down_copies[j].start()
+        if p + 2 < parts:
+            for k in range(1, ring):
+                ring_step(p + 2, k)
     x_steps(parts - 1)
     finish(parts - 1)
 
@@ -276,15 +307,15 @@
     for copy in part_copies + hid_copies + down_copies:
         copy.wait_send()
     for p in range(parts):
-        for k in range(ring):
-            if k < ring - 1:
-                ring_copy(p, k).wait_send()
-            x_copy(p, k).wait_send()
         for k in range(2 * ring):
             sib_copy(p, k).wait_send()
-
-
-def block(normed, residual, wout, gate_weight, up_weight, down_weight, mlp_gain, live):
+            if k % ring < ring - 1 and (k < ring or p in swap_first):
+                ring_copy(p, k).wait_send()
+            if k < ring and swaps(p, k):
+                x_copy(p, k).wait_send()
+
+
+def block(normed, residual, wout, wga, gate_weight, up_weight, down_weight, mlp_gain, live):
     n, peers = lax.axis_size("ctx"), lax.axis_size("head")
     ring, parts = n // 4, 2 + peers
     toks, half = residual.shape
@@ -296,10 +327,10 @@
     return pl.pallas_call(
         functools.partial(block_kernel, n, peers),
         out_shape=jax.ShapeDtypeStruct((toks, half), bf),
-        in_specs=[pl.BlockSpec(memory_space=pltpu.VMEM)] * 8,
+        in_specs=[pl.BlockSpec(memory_space=pltpu.VMEM)] * 9,
         out_specs=pl.BlockSpec(memory_space=pltpu.VMEM),
         scratch_shapes=[
-            pltpu.VMEM((deep, units), bf),
+            pltpu.VMEM((deep, units // 2), bf),
             pltpu.VMEM((deep, units), bf),
             pltpu.VMEM((peers, units, half), bf),
             pltpu.VMEM((peers - 1, toks, half), bf),
@@ -310,7 +341,7 @@
             pltpu.VMEM((toks, units), bf),
             pltpu.VMEM((peers - 1, toks, half), bf),
             pltpu.VMEM((peers - 1, toks, half), bf),
-            sems((parts, ring)), sems((parts, ring)),
+            sems((parts, 2 * ring)), sems((parts, 2 * ring)),
             sems((parts, ring)), sems((parts, ring)),
             sems((parts, 2 * ring)), sems((parts, 2 * ring)),
             sems((3, peers - 1)), sems((3, peers - 1)),
@@ -323,7 +354,7 @@
             bytes_accessed=40 * 1024 * 1024,
             transcendentals=toks * units,
         ),
-    )(normed, residual, wout, gate_weight, up_weight, down_weight, mlp_gain, live)
+    )(normed, residual, wout, wga, gate_weight, up_weight, down_weight, mlp_gain, live)
 
 
 def shards(
@@ -347,6 +378,8 @@
     group_total = tok_rows // GROUP
     head_count = log_decay.shape[0]
     wout = lax.all_gather(out_weight, "ctx", axis=0, tiled=True)
+    cut = gate_weight.shape[1] // 2
+    wga = lax.all_gather(gate_weight[:, :cut], "ctx", axis=0, tiled=True)
     masked = mixer_input * live_mask.astype(jnp.bfloat16)[:, None]
     read_groups = read_vecs.reshape(group_total, GROUP, -1)
     group_data = (
@@ -388,6 +421,7 @@
         normed,
         residual,
         wout,
+        wga,
         gate_weight,
         up_weight,
         down_weight,

time: 312 us -> 315 us (level)
  waiting for transfers between devices: 38.6 us -> 63.8 us
  Pallas kernels: 166 us -> 147 us
  starting transfers between devices: 18.2 us -> 11.9 us
    all_gather x1, waiting for transfers between devices: 0.01 us -> 20.7 us  [shards(): wout = lax.all_gather(out_weight, 'ctx', axis=0, tiled=True)]
    pallas_call x1, Pallas kernels: 166 us -> 147 us  [block(): pl.pallas_call(functools.partial(block_kernel, n, peers), out_shape=jax.S...]
    all_to_all x1, waiting for transfers between devices: 13.4 us -> 22 us  [carried_in(): back = lax.all_to_all(jnp.stack(entering), 'ctx', 0, 0)]
    all_to_all x1, starting transfers between devices: 10.8 us -> 4.43 us  [carried_in(): back = lax.all_to_all(jnp.stack(entering), 'ctx', 0, 0)]
    all_to_all x1, waiting for transfers between devices: 24.5 us -> 20.5 us  [carried_in(): packed = lax.all_to_all(packed, 'ctx', 0, 0)]
  transfers between devices with their start and end apart: 3 -> 4, of which waited for: 2 -> 3; matrix products, arithmetic and copies ran while one was open for 21% -> 21% of each run, Pallas kernels for 0% -> 0%
where the time goes in v2:
time: 315 us; the launch traced here: 314 us
  Pallas kernels  147 us (47%)
  waiting for transfers between devices  63.8 us (20%)
  other arithmetic  33.5 us (11%)
  local copies, waits for them, and re-layouts  21.7 us (7%)
  matrix products  15.6 us (5%)
  between operations  13.6 us (4%)
  starting transfers between devices  11.9 us (4%)
  blocking collectives  5.12 us (2%)
    pallas_call x1, Pallas kernels, block(): pl.pallas_call(functools.partial(block_kernel, n, peers), out_shape=jax.S...  147 us
    all_to_all x1, waiting for transfers between devices, carried_in(): back = lax.all_to_all(jnp.stack(entering), 'ctx', 0, 0)  22 us
    all_gather x1, waiting for transfers between devices, shards(): wout = lax.all_gather(out_weight, 'ctx', axis=0, tiled=True)  20.7 us
    all_to_all x1, waiting for transfers between devices, carried_in(): packed = lax.all_to_all(packed, 'ctx', 0, 0)  20.5 us
    unnamed x14, other arithmetic  9.89 us
    dot_general x2, matrix products, group_core(): jnp.einsum('hij,jhp->ihp', weights, per_head, preferred_element_type=jnp....  7.54 us
    all_to_all x1, starting transfers between devices, carried_in(): packed = lax.all_to_all(packed, 'ctx', 0, 0)  7.4 us
  transfers between devices with their start and end apart: 4, of which 3 were waited for; matrix products, arithmetic and copies ran while one was open for 21% of the time, Pallas kernels for 0%

profile of v2, /device:TPU:0, one launch (start us, length us, event | category | flops | bytes accessed | tf_op | source)
XLA Modules:
  0.0 314.2 jit_solution(1313835813770127909)
XLA Ops:
  6.5 1.7 slice.240
  8.3 0.7 all-gather.3.cloned.1.call-update
  9.1 0.8 fusion.57
  9.8 0.9 reshape.1068
  10.7 0.7 reshape.1065
  11.4 3.1 %broadcast_multiply_fusion = bf16[512,2048]{1,0:T(8,128)(2,1)} fusion(bf16[512,2048]{1,0:T(8,128)(2,1)} %param.17, bf16[512]{0:T(512)(128)(2,1)S(1)} %get-tuple-element.164), kind=kLoop, calls=%fused_computation.56 | loop fusion | flops 1048576 | bytes 4195328 | tf_op jit(solution)/shard_map/mul | solution.py:383
  14.6 24.9 %while.16 = (s32[]{:T(128)}, f32[2,256,32,64]{1,3,2,0:T(8,128)}, f32[2,32,64,128]{3,2,1,0:T(8,128)}, f32[2,32,256]{2,1,0:T(8,128)S(1)}, f32[2,32]{1,0:T(2,128)S(...) while((s32[]{:T(128)}, f32[2,256,32,64]{1,3,2,0:T(8,128)}, ...), condition=%wide.region_5.6_spmd, body=%wide.region_0.5_spmd.sunk | while | flops 434922624 | bytes 12338567 | solution.py:396
  16.5 1.3 constant_dynamic-slice_fusion.6
  18.3 3.8 %bitcast_dynamic-update-slice_fusion.2 = f32[2,256,32,64]{1,3,2,0:T(8,128)} fusion(f32[2,256,32,64]{1,3,2,0:T(8,128)} %get-tuple-element.261, s32[]{:T(128)} %get-tuple-element.260, bf16[256,32,64]{0,2,1:T(8,128)(2,1)S(1)} %bitcast.109, f32[32,256]{1,0:T(8,128)S(1)} %bitcast.119, f32[256,256]{1,0:T(8,128)S(1)} %fusion.73, ...), kind=kOutput, calls=%fused_computation.10.clone.1 | convolution fusion | flops 280494080 | bytes 4588544 | tf_op jit(solution)/shard_map/while/body/eval_jaxpr/hij,jhp->ihp/dot_general | solution.py:57
  22.1 0.7 slice.392
  23.6 0.7 compare_convert_fusion.5
  24.4 2.5 fusion.75
  28.9 1.3 constant_dynamic-slice_fusion.6
  30.8 3.8 %bitcast_dynamic-update-slice_fusion.2 = f32[2,256,32,64]{1,3,2,0:T(8,128)} fusion(f32[2,256,32,64]{1,3,2,0:T(8,128)} %get-tuple-element.261, s32[]{:T(128)} %get-tuple-element.260, bf16[256,32,64]{0,2,1:T(8,128)(2,1)S(1)} %bitcast.109, f32[32,256]{1,0:T(8,128)S(1)} %bitcast.119, f32[256,256]{1,0:T(8,128)S(1)} %fusion.73, ...), kind=kOutput, calls=%fused_computation.10.clone.1 | convolution fusion | flops 280494080 | bytes 4588544 | tf_op jit(solution)/shard_map/while/body/eval_jaxpr/hij,jhp->ihp/dot_general | solution.py:57
  34.5 0.7 slice.392
  36.1 0.7 compare_convert_fusion.5
  36.9 2.5 fusion.75
  40.0 1.7 fusion.55
  42.4 0.9 pad_maximum_fusion.1
  43.2 7.4 %all-to-all-start = ((bf16[16,144,128]{2,1,0:T(8,128)(2,1)}), bf16[16,144,128]{2,1,0:T(8,128)(2,1)S(1)}, u32[]{:S(2)}, u32[]{:S(2)}) async-start(bf16[16,144,128]{2,1,0:T(8,128)(2,1)} %pad_maximum_fusion.1), calls=%async_computation | async-start | bytes 1179648 | tf_op jit(solution)/shard_map/all_to_all | solution.py:31
  51.3 20.5 %all-to-all-done = bf16[16,144,128]{2,1,0:T(8,128)(2,1)S(1)} async-done(((bf16[16,144,128]{2,1,0:T(8,128)(2,1)}), bf16[16,144,128]{2,1,0:T(8,128)(2,1)S(1)}, u32[]{:S(2)}, u32[]{:S(2)}) %all-to-all-start) | async-done | bytes 589856 | tf_op jit(solution)/shard_map/all_to_all | solution.py:31
  73.3 0.7 fusion.45
  74.0 0.7 fusion.44
  74.7 0.7 constant_dynamic-update-slice_fusion.5
  75.4 0.7 fusion.43
  76.2 0.8 constant_dynamic-update-slice_fusion.4
  76.9 0.7 fusion.42
  77.6 0.7 constant_dynamic-update-slice_fusion.3
  78.3 0.7 fusion.41
  79.0 0.7 constant_dynamic-update-slice_fusion.2
  79.7 0.7 fusion.40
  80.4 0.7 constant_dynamic-update-slice_fusion.1
  81.1 0.7 fusion.39
  81.8 0.7 constant_dynamic-update-slice_fusion
  82.5 0.7 fusion.38
  83.2 0.7 fusion.46
  83.9 4.4 %all-to-all-start.1 = ((bf16[16,128,128]{2,1,0:T(8,128)(2,1)}), bf16[16,128,128]{2,1,0:T(8,128)(2,1)S(1)}, u32[]{:S(2)}, u32[]{:S(2)}) async-start(bf16[16,128,128]{2,1,0:T(8,128)(2,1)} %fusion.46), calls=%async_computation.1 | async-start | bytes 1048576 | tf_op jit(solution)/shard_map/all_to_all | solution.py:42
  88.5 0.9 copy.60.live
  89.4 22.0 %all-to-all-done.1 = bf16[16,128,128]{2,1,0:T(8,128)(2,1)S(1)} async-done(((bf16[16,128,128]{2,1,0:T(8,128)(2,1)}), bf16[16,128,128]{2,1,0:T(8,128)(2,1)S(1)}, u32[]{:S(2)}, u32[]{:S(2)}) %all-to-all-start.1) | async-done | bytes 524320 | tf_op jit(solution)/shard_map/all_to_all | solution.py:42
  112.0 2.3 fusion.24
  114.8 2.9 pad_maximum_fusion
  117.6 5.6 %copy.59 = f32[512,2048]{1,0:T(8,128)} copy(f32[512,2048]{0,1:T(8,128)} %bitcast.111) | data formatting | bytes 8388608 | tf_op jit(solution)/shard_map/reshape | solution.py:416
  123.2 3.6 %multiply_reduce_fusion.1 = f32[512]{0:T(512)S(1)} fusion(f32[512,2048]{1,0:T(8,128)} %copy.59, bf16[512,2048]{1,0:T(8,128)(2,1)S(1)} %copy-done), kind=kLoop, calls=%fused_computation.49 | loop fusion | flops 8388096 | bytes 6293504 | tf_op jit(solution)/shard_map/reduce_sum | solution.py:418
  126.8 5.1 %psum.7 = f32[512]{0:T(512)S(1)} all-reduce(f32[512]{0:T(512)S(1)} %multiply_reduce_fusion.1), channel_id=1, replica_groups=mesh['ctx'=16,'head'=2] {'head'}, use_global_device_ids=true, to_apply=%region_7.8 | all-reduce | flops 512 | bytes 4096 | tf_op jit(solution)/shard_map/psum | solution.py:418
  131.9 5.2 %multiply_convert_fusion.6.normed = bf16[512,2048]{1,0:T(8,128)(2,1)} fusion(f32[2048]{0:T(1024)S(1)} %copy-done.4, f32[512]{0:T(512)S(1)} %add_rsqrt_fusion, f32[512,2048]{1,0:T(8,128)} %copy.59, bf16[512,2048]{1,0:T(8,128)(2,1)S(1)} %copy-done), kind=kLoop, calls=%fused_computation.48 | loop fusion | flops 9437184 | bytes 8398848 | tf_op jit(solution)/shard_map/convert_element_type | solution.py:419
  137.1 20.7 %all-gather.3.cloned.1.call-done.wout = bf16[2048,2048]{1,0:T(8,128)(2,1)} async-done(((bf16[128,2048]{1,0:T(8,128)(2,1)}), bf16[2048,2048]{1,0:T(8,128)(2,1)}) %all-gather.3.cloned.1.call-update) | async-done | bytes 8388624 | tf_op jit(solution)/shard_map/all_gather | solution.py:380
  157.8 147.3 %shard_map.145 = bf16[512,1024]{1,0:T(8,128)(2,1)} custom-call(bf16[512,2048]{1,0:T(8,128)(2,1)} %multiply_convert_fusion.6.normed, bf16[512,1024]{1,0:T(8,128)(2,1)} %res.1, bf16[2048,2048]{1,0:T(8,128)(2,1)} %all-gather.3.cloned.1.call-done.wout, bf16[2048,1024]{1,0:T(8,128)(2,1)} %all-gather.5.cloned.1.call-done.wga, bf16[128,2048]{1,0:T(8,128)(2,1)} %g_sh.1, ...), custom_call_target="tpu_custom_call" | custom-call | flops 17179869184 | bytes 41943040 | tf_op jit(solution)/shard_map/pallas_call | solution.py:327
  305.1 2.3 copy.115
  (96 shorter events, 10.2 us)
Async XLA Ops:
  6.5 8.0 %copy-start.3 = (bf16[512,128]{1,0:T(8,128)(2,1)S(1)}, bf16[512,128]{1,0:T(8,128)(2,1)}, u32[]{:S(2)}) copy-start(bf16[512,128]{1,0:T(8,128)(2,1)} %param.20) | copy-start | bytes 393220
  6.5 8.0 %copy-start.2 = (bf16[512,128]{1,0:T(8,128)(2,1)S(1)}, bf16[512,128]{1,0:T(8,128)(2,1)}, u32[]{:S(2)}) copy-start(bf16[512,128]{1,0:T(8,128)(2,1)} %param.19) | copy-start | bytes 393220
  6.5 8.0 %copy-start.5 = (f32[32]{0:T(128)S(1)}, f32[32]{0:T(128)}, u32[]{:S(2)}) copy-start(f32[32]{0:T(128)} %param.24) | copy-start | bytes 388
  6.5 130.6 %all-gather.5.cloned.1.call-start = ((), (), s32[]{:S(2)}) async-start(), calls=%async_computation.3 | async-start | bytes 4456448 | tf_op jit(solution)/shard_map/all_gather | solution.py:382
  8.3 149.5 %all-gather.3.cloned.1.call-start = ((), (), s32[]{:S(2)}) async-start(), calls=%async_computation.2 | async-start | bytes 8912896 | tf_op jit(solution)/shard_map/all_gather | solution.py:380
  43.2 28.5 %all-to-all-start = ((bf16[16,144,128]{2,1,0:T(8,128)(2,1)}), bf16[16,144,128]{2,1,0:T(8,128)(2,1)S(1)}, u32[]{:S(2)}, u32[]{:S(2)}) async-start(bf16[16,144,128]{2,1,0:T(8,128)(2,1)} %pad_maximum_fusion.1), calls=%async_computation | async-start | bytes 1179648 | tf_op jit(solution)/shard_map/all_to_all | solution.py:31
  83.9 27.4 %all-to-all-start.1 = ((bf16[16,128,128]{2,1,0:T(8,128)(2,1)}), bf16[16,128,128]{2,1,0:T(8,128)(2,1)S(1)}, u32[]{:S(2)}, u32[]{:S(2)}) async-start(bf16[16,128,128]{2,1,0:T(8,128)(2,1)} %fusion.46), calls=%async_computation.1 | async-start | bytes 1048576 | tf_op jit(solution)/shard_map/all_to_all | solution.py:42
  111.4 3.0 copy-start.1
  117.6 5.6 %copy-start = (bf16[512,2048]{1,0:T(8,128)(2,1)S(1)}, bf16[512,2048]{1,0:T(8,128)(2,1)}, u32[]{:S(2)}) copy-start(bf16[512,2048]{1,0:T(8,128)(2,1)} %param.18) | copy-start | bytes 6291460
  123.2 8.7 %copy-start.4 = (f32[2048]{0:T(1024)S(1)}, f32[2048]{0:T(1024)}, u32[]{:S(2)}) copy-start(f32[2048]{0:T(1024)} %param.25) | copy-start | bytes 24580
Sparse Core Ops, SparseCore 0:
  9.5 62.5 all-gather.4
  74.3 83.5 all-gather.2

commit v3 on v2

--- a/solution.py
+++ b/solution.py
@@ -68,7 +68,7 @@
 
 
 def block_kernel(
-    n, peers, normed, res, wout, wga, g_sh, u_sh, d_sh, gain, live, out,
+    n, peers, normed, res, both, g_sh, u_sh, d_sh, gain, live, out,
     wg, wu, wd, psend, precv, own, hid, scaled, act, dsend, drecv,
     ring_s, ring_r, x_s, x_r, sib_s, sib_r, y_s, y_r,
 ):
@@ -90,7 +90,10 @@
         pl.semaphore_signal(barrier, inc=1, device_id=device, device_id_type=MESH)
     pl.semaphore_wait(barrier, 3 + peers)
 
-    cut = wga.shape[1]
+    width = hid.shape[1]
+    cut = wg.shape[1]
+    wout = both.at[pl.ds(0, normed.shape[1]), pl.ds(0, width)]
+    wga = both.at[:, pl.ds(width, cut)]
     full = [wg, wu] + [wd.at[j] for j in range(peers)]
     shard = [g_sh.at[:, pl.ds(cut, cut)], u_sh] + [d_sh.at[:, pl.ds(start, half)] for start in starts]
     parts = len(full)
@@ -315,11 +318,23 @@
                 x_copy(p, k).wait_send()
 
 
-def block(normed, residual, wout, wga, gate_weight, up_weight, down_weight, mlp_gain, live):
+def gather_both(out_rows, gate_rows):
+    split = gate_rows.shape[0] // out_rows.shape[0]
+    gates = gate_rows.reshape(out_rows.shape[0], -1)
+    whole = lax.all_gather(jnp.concatenate([out_rows, gates], axis=1), "ctx", axis=0, tiled=True)
+    if split == 1:
+        return whole
+    width = out_rows.shape[1]
+    gates = whole[:, width:].reshape(whole.shape[0] * split, -1)
+    outs = jnp.pad(whole[:, :width], ((0, gates.shape[0] - whole.shape[0]), (0, 0)))
+    return jnp.concatenate([outs, gates], axis=1)
+
+
+def block(normed, residual, both, gate_weight, up_weight, down_weight, mlp_gain, live):
     n, peers = lax.axis_size("ctx"), lax.axis_size("head")
     ring, parts = n // 4, 2 + peers
     toks, half = residual.shape
-    width = wout.shape[1]
+    width = half * peers
     deep = gate_weight.shape[0] * n
     units = gate_weight.shape[1]
     bf, f32 = jnp.bfloat16, jnp.float32
@@ -327,7 +342,7 @@
     return pl.pallas_call(
         functools.partial(block_kernel, n, peers),
         out_shape=jax.ShapeDtypeStruct((toks, half), bf),
-        in_specs=[pl.BlockSpec(memory_space=pltpu.VMEM)] * 9,
+        in_specs=[pl.BlockSpec(memory_space=pltpu.VMEM)] * 8,
         out_specs=pl.BlockSpec(memory_space=pltpu.VMEM),
         scratch_shapes=[
             pltpu.VMEM((deep, units // 2), bf),
@@ -354,7 +369,7 @@
             bytes_accessed=40 * 1024 * 1024,
             transcendentals=toks * units,
         ),
-    )(normed, residual, wout, wga, gate_weight, up_weight, down_weight, mlp_gain, live)
+    )(normed, residual, both, gate_weight, up_weight, down_weight, mlp_gain, live)
 
 
 def shards(
@@ -377,9 +392,8 @@
     tok_rows = mixer_input.shape[0]
     group_total = tok_rows // GROUP
     head_count = log_decay.shape[0]
-    wout = lax.all_gather(out_weight, "ctx", axis=0, tiled=True)
     cut = gate_weight.shape[1] // 2
-    wga = lax.all_gather(gate_weight[:, :cut], "ctx", axis=0, tiled=True)
+    both = gather_both(out_weight, gate_weight[:, :cut])
     masked = mixer_input * live_mask.astype(jnp.bfloat16)[:, None]
     read_groups = read_vecs.reshape(group_total, GROUP, -1)
     group_data = (
@@ -420,8 +434,7 @@
     return block(
         normed,
         residual,
-        wout,
-        wga,
+        both,
         gate_weight,
         up_weight,
         down_weight,

time: 315 us -> 302 us (0.959)
  waiting for transfers between devices: 63.8 us -> 42.2 us
  starting transfers between devices: 11.9 us -> 20.2 us
    all_gather x2 -> x1, waiting for transfers between devices: 20.7 us -> 0.01 us  [gather_both(): lax.all_gather(jnp.concatenate([out_rows, gates], axis=1), 'ctx', axis=0,...]
    all_to_all x1, starting transfers between devices: 4.43 us -> 12.8 us  [carried_in(): back = lax.all_to_all(jnp.stack(entering), 'ctx', 0, 0)]
  transfers between devices with their start and end apart: 4 -> 3, of which waited for: 3 -> 2; matrix products, arithmetic and copies ran while one was open for 21% -> 22% of each run, Pallas kernels for 0% -> 0%
where the time goes in v3:
time: 302 us; the launch traced here: 301 us
  Pallas kernels  148 us (49%)
  waiting for transfers between devices  42.2 us (14%)
  other arithmetic  33.3 us (11%)
  local copies, waits for them, and re-layouts  21.2 us (7%)
  starting transfers between devices  20.2 us (7%)
  matrix products  15.8 us (5%)
  between operations  13.6 us (5%)
  blocking collectives  5.12 us (2%)
    pallas_call x1, Pallas kernels, block(): pl.pallas_call(functools.partial(block_kernel, n, peers), out_shape=jax.S...  148 us
    all_to_all x1, waiting for transfers between devices, carried_in(): back = lax.all_to_all(jnp.stack(entering), 'ctx', 0, 0)  22 us
    all_to_all x1, waiting for transfers between devices, carried_in(): packed = lax.all_to_all(packed, 'ctx', 0, 0)  20.1 us
    all_to_all x1, starting transfers between devices, carried_in(): back = lax.all_to_all(jnp.stack(entering), 'ctx', 0, 0)  12.8 us
    unnamed x14, other arithmetic  9.87 us
    dot_general x2, matrix products, group_core(): jnp.einsum('hij,jhp->ihp', weights, per_head, preferred_element_type=jnp....  7.54 us
    all_to_all x1, starting transfers between devices, carried_in(): packed = lax.all_to_all(packed, 'ctx', 0, 0)  7.37 us
  transfers between devices with their start and end apart: 3, of which 2 were waited for; matrix products, arithmetic and copies ran while one was open for 22% of the time, Pallas kernels for 0%

profile of v3, /device:TPU:0, one launch (start us, length us, event | category | flops | bytes accessed | tf_op | source)
XLA Modules:
  0.0 301.1 jit_solution(7389318310360317223)
XLA Ops:
  6.6 1.1 slice.240
  7.7 2.0 pad_maximum_fusion.1
  9.8 0.9 reshape.1068
  10.6 0.7 reshape.1065
  11.3 0.8 fusion.57
  12.1 1.6 broadcast_multiply_fusion
  13.7 24.5 %while.16 = (s32[]{:T(128)}, f32[2,256,32,64]{1,3,2,0:T(8,128)}, f32[2,32,64,128]{3,2,1,0:T(8,128)}, f32[2,32,256]{2,1,0:T(8,128)S(1)}, f32[2,32]{1,0:T(2,128)S(...) while((s32[]{:T(128)}, f32[2,256,32,64]{1,3,2,0:T(8,128)}, ...), condition=%wide.region_5.6_spmd, body=%wide.region_0.5_spmd.sunk | while | flops 434922624 | bytes 12338567 | solution.py:410
  15.6 1.3 constant_dynamic-slice_fusion.6
  17.4 3.8 %bitcast_dynamic-update-slice_fusion.2 = f32[2,256,32,64]{1,3,2,0:T(8,128)} fusion(f32[2,256,32,64]{1,3,2,0:T(8,128)} %get-tuple-element.261, s32[]{:T(128)} %get-tuple-element.260, bf16[256,32,64]{0,2,1:T(8,128)(2,1)S(1)} %bitcast.109, f32[32,256]{1,0:T(8,128)S(1)} %bitcast.119, f32[256,256]{1,0:T(8,128)S(1)} %fusion.73, ...), kind=kOutput, calls=%fused_computation.10.clone.1 | convolution fusion | flops 280494080 | bytes 4588544 | tf_op jit(solution)/shard_map/while/body/eval_jaxpr/hij,jhp->ihp/dot_general | solution.py:57
  21.2 0.6 slice.392
  22.6 0.6 compare_convert_fusion.5
  23.4 2.5 fusion.75
  27.9 1.3 constant_dynamic-slice_fusion.6
  29.7 3.8 %bitcast_dynamic-update-slice_fusion.2 = f32[2,256,32,64]{1,3,2,0:T(8,128)} fusion(f32[2,256,32,64]{1,3,2,0:T(8,128)} %get-tuple-element.261, s32[]{:T(128)} %get-tuple-element.260, bf16[256,32,64]{0,2,1:T(8,128)(2,1)S(1)} %bitcast.109, f32[32,256]{1,0:T(8,128)S(1)} %bitcast.119, f32[256,256]{1,0:T(8,128)S(1)} %fusion.73, ...), kind=kOutput, calls=%fused_computation.10.clone.1 | convolution fusion | flops 280494080 | bytes 4588544 | tf_op jit(solution)/shard_map/while/body/eval_jaxpr/hij,jhp->ihp/dot_general | solution.py:57
  34.9 0.6 compare_convert_fusion.5
  35.6 2.5 fusion.75
  38.8 1.7 fusion.55
  41.1 0.8 pad_maximum_fusion.2
  41.9 7.4 %all-to-all-start = ((bf16[16,144,128]{2,1,0:T(8,128)(2,1)}), bf16[16,144,128]{2,1,0:T(8,128)(2,1)S(1)}, u32[]{:S(2)}, u32[]{:S(2)}) async-start(bf16[16,144,128]{2,1,0:T(8,128)(2,1)} %pad_maximum_fusion.2), calls=%async_computation | async-start | bytes 1179648 | tf_op jit(solution)/shard_map/all_to_all | solution.py:31
  50.0 20.1 %all-to-all-done = bf16[16,144,128]{2,1,0:T(8,128)(2,1)S(1)} async-done(((bf16[16,144,128]{2,1,0:T(8,128)(2,1)}), bf16[16,144,128]{2,1,0:T(8,128)(2,1)S(1)}, u32[]{:S(2)}, u32[]{:S(2)}) %all-to-all-start) | async-done | bytes 589856 | tf_op jit(solution)/shard_map/all_to_all | solution.py:31
  70.3 0.7 gather_fusion
  71.0 0.6 slice_reduce_fusion.3
  71.7 0.7 fusion.45
  72.4 0.7 fusion.44
  73.1 0.7 constant_dynamic-update-slice_fusion.5
  73.8 0.7 fusion.43
  74.5 0.8 constant_dynamic-update-slice_fusion.4
  75.3 0.7 fusion.42
  76.0 0.7 constant_dynamic-update-slice_fusion.3
  76.7 0.7 fusion.41
  77.4 0.7 constant_dynamic-update-slice_fusion.2
  78.1 0.7 fusion.40
  78.7 0.7 constant_dynamic-update-slice_fusion.1
  79.4 0.7 fusion.39
  80.1 0.7 constant_dynamic-update-slice_fusion
  80.9 0.7 fusion.38
  81.5 0.7 fusion.46
  82.3 12.8 %all-to-all-start.1 = ((bf16[16,128,128]{2,1,0:T(8,128)(2,1)}), bf16[16,128,128]{2,1,0:T(8,128)(2,1)S(1)}, u32[]{:S(2)}, u32[]{:S(2)}) async-start(bf16[16,128,128]{2,1,0:T(8,128)(2,1)} %fusion.46), calls=%async_computation.1 | async-start | bytes 1048576 | tf_op jit(solution)/shard_map/all_to_all | solution.py:42
  95.2 0.9 copy.60.live
  96.1 22.0 %all-to-all-done.1 = bf16[16,128,128]{2,1,0:T(8,128)(2,1)S(1)} async-done(((bf16[16,128,128]{2,1,0:T(8,128)(2,1)}), bf16[16,128,128]{2,1,0:T(8,128)(2,1)S(1)}, u32[]{:S(2)}, u32[]{:S(2)}) %all-to-all-start.1) | async-done | bytes 524320 | tf_op jit(solution)/shard_map/all_to_all | solution.py:42
  118.7 2.5 fusion.24
  121.7 2.5 pad_maximum_fusion
  124.2 5.6 %copy.59 = f32[512,2048]{1,0:T(8,128)} copy(f32[512,2048]{0,1:T(8,128)} %bitcast.111) | data formatting | bytes 8388608 | tf_op jit(solution)/shard_map/reshape | solution.py:430
  129.8 3.6 %multiply_reduce_fusion.1 = f32[512]{0:T(512)S(1)} fusion(f32[512,2048]{1,0:T(8,128)} %copy.59, bf16[512,2048]{1,0:T(8,128)(2,1)S(1)} %copy-done), kind=kLoop, calls=%fused_computation.49 | loop fusion | flops 8388096 | bytes 6293504 | tf_op jit(solution)/shard_map/reduce_sum | solution.py:432
  133.4 5.1 %psum.7 = f32[512]{0:T(512)S(1)} all-reduce(f32[512]{0:T(512)S(1)} %multiply_reduce_fusion.1), channel_id=1, replica_groups=mesh['ctx'=16,'head'=2] {'head'}, use_global_device_ids=true, to_apply=%region_7.8 | all-reduce | flops 512 | bytes 4096 | tf_op jit(solution)/shard_map/psum | solution.py:432
  138.5 5.2 %multiply_convert_fusion.6.normed = bf16[512,2048]{1,0:T(8,128)(2,1)} fusion(f32[2048]{0:T(1024)S(1)} %copy-done.5, f32[512]{0:T(512)S(1)} %add_rsqrt_fusion, f32[512,2048]{1,0:T(8,128)} %copy.59, bf16[512,2048]{1,0:T(8,128)(2,1)S(1)} %copy-done), kind=kLoop, calls=%fused_computation.48 | loop fusion | flops 9437184 | bytes 8398848 | tf_op jit(solution)/shard_map/convert_element_type | solution.py:433
  143.7 148.3 %shard_map.145 = bf16[512,1024]{1,0:T(8,128)(2,1)} custom-call(bf16[512,2048]{1,0:T(8,128)(2,1)} %multiply_convert_fusion.6.normed, bf16[512,1024]{1,0:T(8,128)(2,1)} %res.1, bf16[2048,3072]{1,0:T(8,128)(2,1)} %all-gather.2.cloned.1.call-done.both, bf16[128,2048]{1,0:T(8,128)(2,1)} %g_sh.1, bf16[128,2048]{1,0:T(8,128)(2,1)} %u_sh.1, bf16[128,2048]{1,0:T(8,128)(2,1)} %d_sh.1, ...), custom_call_target="tpu_custom_call" | custom-call | flops 17179869184 | bytes 41943040 | tf_op jit(solution)/shard_map/pallas_call | solution.py:342
  292.0 2.3 copy.115
  (96 shorter events, 9.5 us)
Async XLA Ops:
  6.5 5.6 %copy-start.3 = (bf16[512,2048]{1,0:T(8,128)(2,1)S(1)}, bf16[512,2048]{1,0:T(8,128)(2,1)}, u32[]{:S(2)}) copy-start(bf16[512,2048]{1,0:T(8,128)(2,1)} %param.17) | copy-start | bytes 6291460
  6.5 7.1 %copy-start.4 = (bf16[512,128]{1,0:T(8,128)(2,1)S(1)}, bf16[512,128]{1,0:T(8,128)(2,1)}, u32[]{:S(2)}) copy-start(bf16[512,128]{1,0:T(8,128)(2,1)} %param.20) | copy-start | bytes 393220
  6.5 7.1 %copy-start.2 = (bf16[512,128]{1,0:T(8,128)(2,1)S(1)}, bf16[512,128]{1,0:T(8,128)(2,1)}, u32[]{:S(2)}) copy-start(bf16[512,128]{1,0:T(8,128)(2,1)} %param.19) | copy-start | bytes 393220
  6.5 7.1 %copy-start.6 = (f32[32]{0:T(128)S(1)}, f32[32]{0:T(128)}, u32[]{:S(2)}) copy-start(f32[32]{0:T(128)} %param.24) | copy-start | bytes 388
  6.5 137.2 %all-gather.2.cloned.1.call-start = ((), (), s32[]{:S(2)}) async-start(), calls=%async_computation.2 | async-start | bytes 13369344 | tf_op jit(solution)/shard_map/all_gather | solution.py:324
  41.9 28.2 %all-to-all-start = ((bf16[16,144,128]{2,1,0:T(8,128)(2,1)}), bf16[16,144,128]{2,1,0:T(8,128)(2,1)S(1)}, u32[]{:S(2)}, u32[]{:S(2)}) async-start(bf16[16,144,128]{2,1,0:T(8,128)(2,1)} %pad_maximum_fusion.2), calls=%async_computation | async-start | bytes 1179648 | tf_op jit(solution)/shard_map/all_to_all | solution.py:31
  82.3 35.9 %all-to-all-start.1 = ((bf16[16,128,128]{2,1,0:T(8,128)(2,1)}), bf16[16,128,128]{2,1,0:T(8,128)(2,1)S(1)}, u32[]{:S(2)}, u32[]{:S(2)}) async-start(bf16[16,128,128]{2,1,0:T(8,128)(2,1)} %fusion.46), calls=%async_computation.1 | async-start | bytes 1048576 | tf_op jit(solution)/shard_map/all_to_all | solution.py:42
  118.1 3.1 %copy-start.1 = (f32[2,256,32,64]{1,3,2,0:T(8,128)S(1)}, f32[2,256,32,64]{1,3,2,0:T(8,128)}, u32[]{:S(2)}) copy-start(f32[2,256,32,64]{1,3,2,0:T(8,128)} %get-tuple-element.65) | copy-start | bytes 12582916
  124.2 5.6 %copy-start = (bf16[512,2048]{1,0:T(8,128)(2,1)S(1)}, bf16[512,2048]{1,0:T(8,128)(2,1)}, u32[]{:S(2)}) copy-start(bf16[512,2048]{1,0:T(8,128)(2,1)} %param.18) | copy-start | bytes 6291460
  129.8 8.7 %copy-start.5 = (f32[2048]{0:T(1024)S(1)}, f32[2048]{0:T(1024)}, u32[]{:S(2)}) copy-start(f32[2048]{0:T(1024)} %param.25) | copy-start | bytes 24580
Sparse Core Ops, SparseCore 0:
  9.8 120.1 all-gather.1
